TPU v7x, 256 devices: a whole 4x4x8 slice. The times are simulated.
256 devices in a mesh: ens: 4 (over y_hi, core), slab: 64 (over y_lo, z, x).
Axes of the slice: x: 4, y: 4 (y_hi: 2, y_lo: 2; y = y_hi * 2 + y_lo), z: 8, core: 2. Of those that a mesh axis runs over, the one named last changes fastest.
Arguments:
- tracer: float32 [32, 1024, 4096], P('ens', 'slab'), may hold values from -6 to 6
- coefficients: float32 [4, 1024, 4096], P(None, 'slab'), may hold values from -1.5 to 1.5, as said below
- parameters: float32 [32, 4096], P('ens'), may hold values from -6 to 6
- obs_index: int32 [131072], P('slab'), may hold values from 0 to 65535, as said below
- obs_values: float32 [32, 131072], P('ens', 'slab'), may hold values from -6 to 6
- obs_variance: float32 [131072], P('slab'), may hold values from 0.1 to 1
- member_group: int32 [32], replicated, may hold values from 0 to 7, as said below
Outputs:
- final_field: float32 [32, 1024, 4096], P('ens', 'slab')
- updated_params: float32 [32, 4096], P('ens')
Inputs may be any that keep to these rules, and one draw needn't show every extreme that they name: `obs_index`: every slab has an observation at flat index 0 and one at 65535; indices may repeat. `member_group`: every group holds exactly 4 members. `coefficients`: the Courant numbers lie within -0.3 to 0.3, the diffusion number within 0.02 to 0.1.
All inputs are finite; a program needn't handle non-finite values.
Results may differ from a plain program's by a relative error of at most 0.0003.
Values sent between devices are 32-bit elements; how exact they have to be, the bound alone decides.
A program may use at most 128 MiB of HBM per device.

v0:
```python
import math

import jax
import jax.numpy as jnp
from jax import lax
from jax.sharding import PartitionSpec as P

STEPS = 4
GROUPS = 8


def padded_2(block, sides, width):
    for axis, dim in sides:
        count = lax.axis_size(axis)
        forward = [(i, i + 1) for i in range(count - 1)]
        backward = [(target, source) for source, target in forward]
        low = lax.ppermute(
            lax.slice_in_dim(block, block.shape[dim] - width, None, axis=dim), axis, forward
        )
        high = lax.ppermute(lax.slice_in_dim(block, 0, width, axis=dim), axis, backward)
        block = jnp.concatenate([low, block, high], axis=dim)
    return block


def hdot(left, right):
    return jnp.dot(left, right, precision=lax.Precision.HIGHEST, preferred_element_type=jnp.float32)


def minmod(left, right):
    return jnp.where(
        left * right > 0.0, jnp.where(jnp.abs(left) < jnp.abs(right), left, right), 0.0
    )


def upwind(minus_two, minus_one, centre, plus_one, plus_two, speed):
    slope_back = minmod(minus_one - minus_two, centre - minus_one)
    slope_here = minmod(centre - minus_one, plus_one - centre)
    slope_next = minmod(plus_one - centre, plus_two - plus_one)
    forward = centre + 0.5 * slope_here - (minus_one + 0.5 * slope_back)
    backward = plus_one - 0.5 * slope_next - (centre - 0.5 * slope_here)
    return speed * jnp.where(speed > 0.0, forward, backward)


def advance(padded, coefficients, params):
    out_rows = padded.shape[-2] - 4
    along_x = [
        lax.slice_in_dim(padded, offset, offset + out_rows, axis=padded.ndim - 2)
        for offset in range(5)
    ]
    centre = along_x[2]
    along_y = [jnp.roll(centre, shift, axis=-1) for shift in (2, 1, 0, -1, -2)]
    advection = upwind(*along_x, coefficients[0]) + upwind(*along_y, coefficients[1])
    laplace = along_x[1] + along_x[3] + along_y[1] + along_y[3] - 4.0 * centre
    source = jnp.expand_dims(params, -2) * coefficients[3]
    return centre - advection + coefficients[2] * laplace + source


def eliminate(system, right_side):
    order = system.shape[0]
    augmented = jnp.concatenate([system, right_side], axis=1)
    positions = jnp.arange(order, dtype=jnp.int32)

    def one_pivot(pivot, current):
        pivot_row = lax.dynamic_slice_in_dim(current, pivot, 1, 0)
        pivot_col = lax.dynamic_slice_in_dim(current, pivot, 1, 1)
        pivot_val = lax.dynamic_slice_in_dim(pivot_row, pivot, 1, 1)
        scaled_row = pivot_row / pivot_val
        is_pivot = (positions == pivot).astype(jnp.float32)[:, None]
        factors = pivot_col * (1.0 - is_pivot)
        current = current - factors * scaled_row
        return current * (1.0 - is_pivot) + is_pivot * scaled_row

    finished = lax.fori_loop(0, order, one_pivot, augmented)
    return finished[:, order:]


def local(tracer, coefficients, parameters, obs_index, obs_values, obs_variance, member_group):
    local_members = tracer.shape[0]
    slab_rows = tracer.shape[1]
    columns = tracer.shape[2]
    ens_pos = lax.axis_index("ens")
    slab_count = lax.axis_size("slab")
    field_now = tracer
    for step_index in range(STEPS):
        padded = padded_2(field_now, (("slab", 1),), 2)
        field_now = advance(padded, coefficients, parameters)
    flat_state = field_now.reshape(local_members, slab_rows * columns)
    predicted = jnp.take(flat_state, obs_index, axis=1)
    total_obs = obs_variance.shape[0] * slab_count
    weight = 1.0 / (obs_variance * total_obs)
    innovation = (obs_values - predicted) * weight[None, :]
    all_predicted, all_params = (
        lax.all_gather(predicted, "ens", axis=0, tiled=True),
        lax.all_gather(parameters, "ens", axis=0, tiled=True),
    )
    members = member_group.shape[0]
    same_group = (member_group[:, None] == member_group[None, :]).astype(jnp.float32)
    per_group = members // GROUPS
    spread = 1.0 / math.sqrt(per_group - 1)
    anomalies = (all_predicted - hdot(same_group, all_predicted) / per_group) * spread
    weighted = anomalies * weight[None, :]
    gram_part = hdot(weighted, anomalies.T)
    mixed_part = hdot(anomalies, innovation.T)
    gram_sum, mixed_sum = lax.psum((gram_part, mixed_part), "slab")
    own_same = lax.dynamic_slice_in_dim(same_group, ens_pos * local_members, local_members, 1)
    system = jnp.eye(members, dtype=jnp.float32) + same_group * gram_sum
    solved = eliminate(system, own_same * mixed_sum)
    param_anomalies = (all_params - hdot(same_group, all_params) / per_group) * spread
    updated_params = parameters + hdot(solved.T, param_anomalies)
    return (field_now, updated_params)


def solution(mesh):
    in_specs = (
        P("ens", "slab", None),
        P(None, "slab", None),
        P("ens", None),
        P("slab"),
        P("ens", "slab"),
        P("slab"),
        P(),
    )
    out_specs = (P("ens", "slab", None), P("ens", None))
    return jax.shard_map(local, mesh=mesh, in_specs=in_specs, out_specs=out_specs, check_vma=False)
```

profile of v0, /device:TPU:24, one launch (start us, length us, event | category | flops | bytes accessed | tf_op | source)
XLA Modules:
  0.0 534.0 jit_solution(13967746560776432302)
XLA Ops:
  0.6 1.8 fusion.75
  3.3 3.4 collective-permute-start
  7.6 8.6 %collective-permute-start.1 = (f32[8,2,4096]{2,0,1:T(8,128)}, f32[8,2,4096]{2,0,1:T(8,128)}, u32[]{:S(2)}, u32[]{:S(2)}) collective-permute-start(f32[8,2,4096]{2,0,1:T(8,128)} %copy.52), channel_id=1, source_target_pairs={{1,0},{2,1},{3,2},{4,3},{5,4},{6,5},{7,6},{8,7},{9,8},{10,9},{11,1... | collective-permute-start | bytes 786440 | tf_op jit(solution)/shard_map/ppermute | solution.py:20
  20.0 8.6 %all_gather.7 = f32[32,4096]{1,0:T(8,128)} all-gather(f32[8,4096]{1,0:T(8,128)S(1)} %copy-done.5), channel_id=1, replica_groups=mesh['ens'=4,'slab'=64] {'ens'}, dimensions={0}, use_global_device_ids=true | all-gather | bytes 655360 | tf_op jit(solution)/shard_map/all_gather | solution.py:94
  28.6 2.5 copy.45
  31.1 2.6 copy.46
  33.7 2.5 copy.49
  36.3 2.6 copy.50
  40.2 2.6 fusion.5
  43.8 1.2 constant_dynamic-update-slice_fusion
  45.1 1.6 constant_dynamic-update-slice_fusion.2
  46.7 8.8 %multiply_add_fusion.4 = f32[8,16,4096]{2,0,1:T(8,128)S(1)} fusion(f32[8,16,2]{2,0,1:T(8,128)S(1)} %copy.44, f32[8,16,4094]{2,0,1:T(8,128)S(1)} %copy-done.1, f32[8,16,4094]{2,0,1:T(8,128)S(1)} %copy-done.2, f32[8,16,2]{2,0,1:T(8,128)S(1)} %copy.47, f32[8,16,1]{2,0,1:T(8,128)} %copy.48, f32[8,16,4095]{2,0,1:T(8,128)S(1)} %copy-done.3, ...), kind=kLoop, calls=%fused_computation.12 | loop fusion | flops 43515904 | bytes 22282240 | tf_op jit(solution)/shard_map/add | solution.py:55
  57.0 1.9 collective-permute-start.2
  58.9 8.4 %collective-permute-start.3 = (f32[8,2,4096]{2,0,1:T(8,128)S(1)}, f32[8,2,4096]{2,0,1:T(8,128)S(1)}, u32[]{:S(2)}, u32[]{:S(2)}) collective-permute-start(f32[8,2,4096]{2,0,1:T(8,128)S(1)} %get-tuple-element.140), channel_id=1, source_target_pairs={{1,0},{2,1},{3,2},{4,3},{5,4},{6,5},{7,6},{8,7},{9,8},{10,9},{11,1... | collective-permute-start | bytes 786440 | tf_op jit(solution)/shard_map/ppermute | solution.py:20
  67.4 4.2 collective-permute-done.2
  71.6 1.2 collective-permute-done.3
  72.8 8.5 %multiply_add_fusion.3 = f32[8,16,4096]{2,0,1:T(8,128)S(1)} fusion(f32[8,16,4096]{2,0,1:T(8,128)S(1)} %multiply_add_fusion.4, f32[8,16,2]{2,0,1:T(8,128)S(1)} %get-tuple-element.146, f32[8,16,4094]{2,0,1:T(8,128)S(1)} %get-tuple-element.148, f32[8,16,4094]{2,0,1:T(8,128)S(1)} %get-tuple-element.147, f32[8,16,2]{2,0,1:T(8,128)S(1)} %get-tuple-element.145, ...), kind=kLoop, calls=%fused_computation.11 | loop fusion | flops 45613056 | bytes 14417920 | tf_op jit(solution)/shard_map/add | solution.py:55
  82.8 1.9 collective-permute-start.4
  84.7 8.6 %collective-permute-start.5 = (f32[8,2,4096]{2,0,1:T(8,128)S(1)}, f32[8,2,4096]{2,0,1:T(8,128)S(1)}, u32[]{:S(2)}, u32[]{:S(2)}) collective-permute-start(f32[8,2,4096]{2,0,1:T(8,128)S(1)} %get-tuple-element.130), channel_id=1, source_target_pairs={{1,0},{2,1},{3,2},{4,3},{5,4},{6,5},{7,6},{8,7},{9,8},{10,9},{11,1... | collective-permute-start | bytes 786440 | tf_op jit(solution)/shard_map/ppermute | solution.py:20
  93.5 3.6 collective-permute-done.4
  97.1 1.2 collective-permute-done.5
  98.3 8.5 %multiply_add_fusion.2 = f32[8,16,4096]{2,0,1:T(8,128)S(1)} fusion(f32[8,16,4096]{2,0,1:T(8,128)S(1)} %multiply_add_fusion.3, f32[8,16,2]{2,0,1:T(8,128)S(1)} %get-tuple-element.136, f32[8,16,4094]{2,0,1:T(8,128)S(1)} %get-tuple-element.138, f32[8,16,4094]{2,0,1:T(8,128)S(1)} %get-tuple-element.137, f32[8,16,2]{2,0,1:T(8,128)S(1)} %get-tuple-element.135, ...), kind=kLoop, calls=%fused_computation.10 | loop fusion | flops 45613056 | bytes 14417920 | tf_op jit(solution)/shard_map/add | solution.py:55
  108.3 1.9 collective-permute-start.6
  110.2 8.6 %collective-permute-start.7 = (f32[8,2,4096]{2,0,1:T(8,128)S(1)}, f32[8,2,4096]{2,0,1:T(8,128)S(1)}, u32[]{:S(2)}, u32[]{:S(2)}) collective-permute-start(f32[8,2,4096]{2,0,1:T(8,128)S(1)} %get-tuple-element.120), channel_id=1, source_target_pairs={{1,0},{2,1},{3,2},{4,3},{5,4},{6,5},{7,6},{8,7},{9,8},{10,9},{11,1... | collective-permute-start | bytes 786440 | tf_op jit(solution)/shard_map/ppermute | solution.py:20
  119.0 2.7 collective-permute-done.6
  122.9 8.5 %multiply_add_fusion.1 = f32[8,16,4096]{2,0,1:T(8,128)S(1)} fusion(f32[8,16,4096]{2,0,1:T(8,128)S(1)} %multiply_add_fusion.2, f32[8,16,2]{2,0,1:T(8,128)S(1)} %get-tuple-element.126, f32[8,16,4094]{2,0,1:T(8,128)S(1)} %get-tuple-element.128, f32[8,16,4094]{2,0,1:T(8,128)S(1)} %get-tuple-element.127, f32[8,16,2]{2,0,1:T(8,128)S(1)} %get-tuple-element.125, ...), kind=kLoop, calls=%fused_computation.9 | loop fusion | flops 45613056 | bytes 14417920 | tf_op jit(solution)/shard_map/add | solution.py:55
  131.4 15.6 %copy.35 = f32[8,16,4096]{0,2,1:T(8,128)} copy(f32[8,16,4096]{2,0,1:T(8,128)S(1)} %multiply_add_fusion.1) | data formatting | bytes 4194304 | tf_op jit(solution)/shard_map/add | solution.py:55
  147.0 2.5 copy.39
  149.5 16.1 %gather_fusion = f32[2048,8]{1,0:T(8,128)S(1)} fusion(f32[8,65536]{0,1:T(8,128)} %bitcast.31, s32[2048]{0:T(1024)S(1)} %copy-done.10), kind=kCustom, calls=%fused_computation | custom fusion | bytes 139264 | tf_op jit(solution)/shard_map/jit(_take)/gather | solution.py:88
  165.9 7.3 %all_gather.6 = f32[32,2048]{1,0:T(8,128)S(1)} all-gather(f32[8,2048]{1,0:T(8,128)S(1)} %select_bitcast_fusion), channel_id=1, replica_groups=mesh['ens'=4,'slab'=64] {'ens'}, dimensions={0}, use_global_device_ids=true | all-gather | bytes 327680 | tf_op jit(solution)/shard_map/all_gather | solution.py:93
  174.2 309.5 %all-reduce = (f32[32,8]{1,0:T(8,128)S(1)}, f32[32,32]{1,0:T(8,128)S(1)}) all-reduce(f32[32,8]{1,0:T(8,128)S(1)} %fusion.41, f32[32,32]{1,0:T(8,128)S(1)} %fusion.39), channel_id=1, replica_groups=mesh['ens'=4,'slab'=64] {'slab'}, use_global_device_ids=true, to_apply=%region_1.2 | all-reduce | flops 1280 | bytes 10240 | tf_op jit(solution)/shard_map/psum | solution.py:104
  484.0 48.9 %while.17 = (s32[]{:T(128)}, f32[32,40]{0,1:T(8,128)S(1)}, s32[]{:T(128)}, s32[]{:T(128)}, s32[]{:T(128)}, /*index=5*/s32[]{:T(128)}) while((s32[]{:T(128)}, f32[32,40]{0,1:T(8,128)S(1)}, s32[]{:T(128)}, s32[]{:T(128)}, s32[]{:T(128)}, /*index=5*/s32[]{:T(128)}) %tuple.74), condition=%wide.region_3.4_spmd.clone, body=%wide.region_2.3_spmd.clone.sunk | while | flops 6732 | bytes 12769 | solution.py:73
  (267 shorter events, 64.6 us)
Async XLA Ops:
  0.6 15.6 %copy-start.6 = (f32[4,16,4096]{2,1,0:T(8,128)S(1)}, f32[4,16,4096]{2,1,0:T(8,128)}, u32[]{:S(2)}) copy-start(f32[4,16,4096]{2,1,0:T(8,128)} %param.10) | copy-start | bytes 3145732
  2.5 13.9 %copy-start = (f32[8,16,4096]{2,1,0:T(8,128)S(1)}, f32[8,16,4096]{2,1,0:T(8,128)}, u32[]{:S(2)}) copy-start(f32[8,16,4096]{2,1,0:T(8,128)} %param.9) | copy-start | bytes 6291460
  3.3 39.5 %collective-permute-start = (f32[8,2,4096]{2,0,1:T(8,128)}, f32[8,2,4096]{2,0,1:T(8,128)}, u32[]{:S(2)}, u32[]{:S(2)}) collective-permute-start(f32[8,2,4096]{2,0,1:T(8,128)} %copy.53), channel_id=1, source_target_pairs={{0,1},{1,2},{2,3},{3,4},{4,5},{5,6},{6,7},{7,8},{8,9},{9,10},{10,1... | collective-permute-start | bytes 786440 | tf_op jit(solution)/shard_map/ppermute | solution.py:17
  7.6 37.5 %collective-permute-start.1 = (f32[8,2,4096]{2,0,1:T(8,128)}, f32[8,2,4096]{2,0,1:T(8,128)}, u32[]{:S(2)}, u32[]{:S(2)}) collective-permute-start(f32[8,2,4096]{2,0,1:T(8,128)} %copy.52), channel_id=1, source_target_pairs={{1,0},{2,1},{3,2},{4,3},{5,4},{6,5},{7,6},{8,7},{9,8},{10,9},{11,1... | collective-permute-start | bytes 786440 | tf_op jit(solution)/shard_map/ppermute | solution.py:20
  17.1 0.9 copy-start.12
  17.2 2.1 copy-start.14
  17.2 2.7 copy-start.9
  17.2 2.8 copy-start.5
  40.2 6.4 %copy-start.4 = (f32[8,16,4095]{2,0,1:T(8,128)S(1)}, f32[8,16,4095]{2,0,1:T(8,128)}, u32[]{:S(2)}) copy-start(f32[8,16,4095]{2,0,1:T(8,128)} %copy.50) | copy-start | bytes 6289924
  43.8 2.9 copy-start.1
  43.8 2.8 copy-start.2
  43.8 2.8 copy-start.3
  57.0 14.7 %collective-permute-start.2 = (f32[8,2,4096]{2,0,1:T(8,128)S(1)}, f32[8,2,4096]{2,0,1:T(8,128)S(1)}, u32[]{:S(2)}, u32[]{:S(2)}) collective-permute-start(f32[8,2,4096]{2,0,1:T(8,128)S(1)} %get-tuple-element.139), channel_id=1, source_target_pairs={{0,1},{1,2},{2,3},{3,4},{4,5},{5,6},{6,7},{7,8},{8,9},{9,10},{10,1... | collective-permute-start | bytes 786440 | tf_op jit(solution)/shard_map/ppermute | solution.py:17
  58.9 13.9 %collective-permute-start.3 = (f32[8,2,4096]{2,0,1:T(8,128)S(1)}, f32[8,2,4096]{2,0,1:T(8,128)S(1)}, u32[]{:S(2)}, u32[]{:S(2)}) collective-permute-start(f32[8,2,4096]{2,0,1:T(8,128)S(1)} %get-tuple-element.140), channel_id=1, source_target_pairs={{1,0},{2,1},{3,2},{4,3},{5,4},{6,5},{7,6},{8,7},{9,8},{10,9},{11,1... | collective-permute-start | bytes 786440 | tf_op jit(solution)/shard_map/ppermute | solution.py:20
  82.8 14.3 %collective-permute-start.4 = (f32[8,2,4096]{2,0,1:T(8,128)S(1)}, f32[8,2,4096]{2,0,1:T(8,128)S(1)}, u32[]{:S(2)}, u32[]{:S(2)}) collective-permute-start(f32[8,2,4096]{2,0,1:T(8,128)S(1)} %get-tuple-element.129), channel_id=1, source_target_pairs={{0,1},{1,2},{2,3},{3,4},{4,5},{5,6},{6,7},{7,8},{8,9},{9,10},{10,1... | collective-permute-start | bytes 786440 | tf_op jit(solution)/shard_map/ppermute | solution.py:17
  84.7 13.6 %collective-permute-start.5 = (f32[8,2,4096]{2,0,1:T(8,128)S(1)}, f32[8,2,4096]{2,0,1:T(8,128)S(1)}, u32[]{:S(2)}, u32[]{:S(2)}) collective-permute-start(f32[8,2,4096]{2,0,1:T(8,128)S(1)} %get-tuple-element.130), channel_id=1, source_target_pairs={{1,0},{2,1},{3,2},{4,3},{5,4},{6,5},{7,6},{8,7},{9,8},{10,9},{11,1... | collective-permute-start | bytes 786440 | tf_op jit(solution)/shard_map/ppermute | solution.py:20
  108.3 13.4 %collective-permute-start.6 = (f32[8,2,4096]{2,0,1:T(8,128)S(1)}, f32[8,2,4096]{2,0,1:T(8,128)S(1)}, u32[]{:S(2)}, u32[]{:S(2)}) collective-permute-start(f32[8,2,4096]{2,0,1:T(8,128)S(1)} %get-tuple-element.119), channel_id=1, source_target_pairs={{0,1},{1,2},{2,3},{3,4},{4,5},{5,6},{6,7},{7,8},{8,9},{9,10},{10,1... | collective-permute-start | bytes 786440 | tf_op jit(solution)/shard_map/ppermute | solution.py:17
  110.2 12.6 %collective-permute-start.7 = (f32[8,2,4096]{2,0,1:T(8,128)S(1)}, f32[8,2,4096]{2,0,1:T(8,128)S(1)}, u32[]{:S(2)}, u32[]{:S(2)}) collective-permute-start(f32[8,2,4096]{2,0,1:T(8,128)S(1)} %get-tuple-element.120), channel_id=1, source_target_pairs={{1,0},{2,1},{3,2},{4,3},{5,4},{6,5},{7,6},{8,7},{9,8},{10,9},{11,1... | collective-permute-start | bytes 786440 | tf_op jit(solution)/shard_map/ppermute | solution.py:20
  146.9 2.5 copy-start.10
  146.9 18.9 %copy-start.13 = (pred[2048]{0:T(1024)(128)(4,1)S(1)}, pred[2048]{0:T(1024)(128)(4,1)}, u32[]{:S(2)}) copy-start(pred[2048]{0:T(1024)(128)(4,1)} %compare_and_fusion) | copy-start | bytes 6148
  149.5 24.4 %copy-start.8 = (f32[8,2048]{1,0:T(8,128)S(1)}, f32[8,2048]{1,0:T(8,128)}, u32[]{:S(2)}) copy-start(f32[8,2048]{1,0:T(8,128)} %param.13) | copy-start | bytes 196612
  149.5 24.4 %copy-start.11 = (f32[2048]{0:T(1024)S(1)}, f32[2048]{0:T(1024)}, u32[]{:S(2)}) copy-start(f32[2048]{0:T(1024)} %get-tuple-element.168) | copy-start | bytes 24580
  149.5 383.5 %copy-start.7 = (f32[32,4096]{1,0:T(8,128)S(1)}, f32[32,4096]{1,0:T(8,128)}, u32[]{:S(2)}) copy-start(f32[32,4096]{1,0:T(8,128)} %fusion.5) | copy-start | bytes 1572868
where the time goes:
time: 535 us; the launch traced here: 534 us
  blocking collectives  325 us (61%)
  local copies, waits for them, and re-layouts  78.8 us (15%)
  other arithmetic  66 us (12%)
  starting transfers between devices  43.4 us (8%)
  waiting for transfers between devices  14 us (3%)
    psum x1, blocking collectives, local(): gram_sum, mixed_sum = lax.psum((gram_part, mixed_part), 'slab')  310 us
    add x4, other arithmetic, advance(): return centre - advection + coefficients[2] * laplace + source  34.3 us
    ppermute x4, starting transfers between devices, padded_2(): lax.ppermute(lax.slice_in_dim(block, 0, width, axis=dim), axis, backward)  34.2 us
    div x32, other arithmetic, one_pivot(): scaled_row = pivot_row / pivot_val  26.3 us
    dynamic_slice x32, local copies, waits for them, and re-layouts, one_pivot(): pivot_val = lax.dynamic_slice_in_dim(pivot_row, pivot, 1, 1)  18.7 us
    unnamed x43, local copies, waits for them, and re-layouts  17 us
    gather x2, local copies, waits for them, and re-layouts, local(): predicted = jnp.take(flat_state, obs_index, axis=1)  16.4 us
    add x1, local copies, waits for them, and re-layouts, advance(): return centre - advection + coefficients[2] * laplace + source  15.6 us
  transfers between devices with their start and end apart: 8, of which 6 were waited for; matrix products, arithmetic and copies ran while one was open for 4% of the time, Pallas kernels for 0%

commit v1 on v0

v1 whole, which is shorter than its diff:
```python
import functools
import math

import jax
import jax.numpy as jnp
from jax import lax
from jax.experimental import pallas as pl
from jax.experimental.pallas import tpu as pltpu
from jax.sharding import PartitionSpec as P

STEPS = 4
GROUPS = 8
LANES = 128
CHUNKS = 4
NEAR = 4
MESH = pl.DeviceIdType.MESH
F32 = jnp.float32
PAIRS = [(a, b) for a in range(4) for b in range(a, 4)]


def lanes_of():
    return lax.broadcasted_iota(jnp.int32, (8, LANES), 1)


def sublanes_of():
    return lax.broadcasted_iota(jnp.int32, (8, LANES), 0)


def half_minmod(left, right):
    return 0.5 * jnp.maximum(jnp.minimum(left, right), jnp.minimum(jnp.maximum(left, right), 0.0))


def across_rows(rows, speeds, spreads, bases):
    count = len(rows) - 4
    diffs = [rows[i + 1] - rows[i] for i in range(count + 3)]
    halves = [half_minmod(diffs[i], diffs[i + 1]) for i in range(count + 2)]
    upper = [rows[i + 1] + halves[i] for i in range(count + 2)]
    lower = [rows[i + 1] - halves[i] for i in range(count + 2)]
    out = []
    for i in range(count):
        speed = speeds[i]
        change = jnp.where(speed > 0.0, upper[i + 1] - upper[i], lower[i + 2] - lower[i + 1])
        out.append(bases[i] - speed * change + spreads[i] * (diffs[i + 2] - diffs[i + 1]))
    return out


def kernel(
    slabs,
    tiles,
    group_ref,
    index_ref,
    tracer_ref,
    coef_ref,
    params_ref,
    values_ref,
    variance_ref,
    field_out,
    params_out,
    tracer_v,
    coef_v,
    own_params,
    variance_v,
    cells,
    halo,
    speed_x,
    speed_y,
    spread,
    source,
    partial_c,
    final_c,
    field_v,
    all_params,
    all_values,
    picked,
    all_picked,
    moved,
    part_near,
    part_far,
    sums_near,
    sums_far,
    load_sem,
    out_sem,
    halo_send,
    halo_recv,
    ens_send,
    ens_recv,
    near_send,
    near_recv,
    far_send,
    far_recv,
):
    ens = lax.axis_index("ens")
    slab = lax.axis_index("slab")
    rows = 16
    per_chunk = tiles // CHUNKS
    far_count = slabs // NEAR
    near_count = 4 * NEAR
    obs_tiles = picked.shape[0]
    quarter = obs_tiles // 4
    has_left = slab > 0
    has_right = slab < slabs - 1
    near_me = ens * NEAR + lax.rem(slab, NEAR)
    far_me = slab // NEAR
    lane = lanes_of()
    first_lane = lane == 0
    last_lane = lane == LANES - 1

    def near_device(i):
        return (i // NEAR, far_me * NEAR + lax.rem(i, NEAR))

    def far_device(i):
        return (ens, i * NEAR + lax.rem(slab, NEAR))

    loads = [
        pltpu.make_async_copy(tracer_ref, tracer_v, load_sem.at[0]),
        pltpu.make_async_copy(coef_ref, coef_v, load_sem.at[1]),
        pltpu.make_async_copy(params_ref, own_params, load_sem.at[2]),
        pltpu.make_async_copy(variance_ref, variance_v, load_sem.at[3]),
        pltpu.make_async_copy(
            values_ref.at[:, pl.ds(pl.multiple_of(ens * (quarter * LANES), LANES), quarter * LANES)],
            all_values.at[ens],
            load_sem.at[4],
        ),
    ]
    for load in loads:
        load.start()

    barrier = pltpu.get_barrier_semaphore()

    @pl.loop(1, near_count)
    def _(p):
        pl.semaphore_signal(
            barrier, inc=1, device_id=near_device(lax.rem(near_me + p, near_count)), device_id_type=MESH
        )

    @pl.loop(1, far_count)
    def _(p):
        pl.semaphore_signal(
            barrier, inc=1, device_id=far_device(lax.rem(far_me + p, far_count)), device_id_type=MESH
        )

    @pl.when(has_left)
    def _():
        pl.semaphore_signal(barrier, inc=1, device_id=(ens, slab - 1), device_id_type=MESH)

    @pl.when(has_right)
    def _():
        pl.semaphore_signal(barrier, inc=1, device_id=(ens, slab + 1), device_id_type=MESH)

    loads[0].wait()

    def of_tile(row, j):
        return (row // 8 * tiles + j) * 8 + row % 8

    def take_row(row):
        for j in range(tiles):
            cells[0, row, j] = tracer_v[pl.ds(of_tile(row, j), 8, stride=rows * tiles), :]

    take_row(0)
    take_row(1)
    take_row(rows - 2)
    take_row(rows - 1)

    zero = jnp.zeros((8, LANES), F32)

    def clear(side):
        @pl.loop(0, STEPS)
        def _(t):
            for r in range(2):
                for j in range(tiles):
                    halo[t, side, r, j] = zero

    pl.when(jnp.logical_not(has_left))(functools.partial(clear, 0))
    pl.when(jnp.logical_not(has_right))(functools.partial(clear, 1))

    neighbours = jnp.where(has_left, 1, 0) + jnp.where(has_right, 1, 0)
    pl.semaphore_wait(barrier, near_count + far_count - 2 + neighbours)

    def halo_copy(t, side, k):
        window = pl.ds(k * per_chunk, per_chunk)
        return pltpu.make_async_remote_copy(
            src_ref=cells.at[t, pl.ds(rows - 2, 2) if side == 0 else pl.ds(0, 2), window],
            dst_ref=halo.at[t, side, :, window],
            send_sem=halo_send.at[t, side, k],
            recv_sem=halo_recv.at[t, side, k],
            device_id=(ens, slab + 1 if side == 0 else slab - 1),
            device_id_type=MESH,
        )

    def send_halo(t, side, k):
        @pl.when(has_right if side == 0 else has_left)
        def _():
            halo_copy(t, side, k).start()

    def wait_halo(t, side, k):
        @pl.when(has_left if side == 0 else has_right)
        def _():
            halo_copy(t, side, k).wait_recv()

    @pl.loop(0, CHUNKS)
    def _(k):
        send_halo(0, 0, k)
        send_halo(0, 1, k)

    loads[2].wait()

    def params_copy(p):
        return pltpu.make_async_remote_copy(
            src_ref=own_params,
            dst_ref=all_params.at[ens],
            send_sem=ens_send.at[0, p],
            recv_sem=ens_recv.at[0, p],
            device_id=(lax.rem(ens + p, 4), slab),
            device_id_type=MESH,
        )

    def values_copy(p):
        target = lax.rem(ens + p, 4)
        return pltpu.make_async_remote_copy(
            src_ref=values_ref.at[:, pl.ds(pl.multiple_of(target * (quarter * LANES), LANES), quarter * LANES)],
            dst_ref=all_values.at[ens],
            send_sem=ens_send.at[1, p],
            recv_sem=ens_recv.at[1, p],
            device_id=(target, slab),
            device_id_type=MESH,
        )

    def picked_copy(p):
        target = lax.rem(ens + p, 4)
        return pltpu.make_async_remote_copy(
            src_ref=picked.at[pl.ds(target * quarter, quarter)],
            dst_ref=all_picked.at[ens],
            send_sem=ens_send.at[2, p],
            recv_sem=ens_recv.at[2, p],
            device_id=(target, slab),
            device_id_type=MESH,
        )

    for p in range(1, 4):
        params_copy(p).start()
        values_copy(p).start()

    for row in range(2, rows - 2):
        take_row(row)

    loads[1].wait()

    @pl.loop(0, tiles)
    def _(j):
        window = pl.ds(pl.multiple_of(j * LANES, LANES), LANES)
        for r in range(rows):
            expanded = [
                jnp.broadcast_to(coef_v[c, pl.ds(r, 1), window], (8, LANES)) for c in range(4)
            ]
            speed_x[r, j] = expanded[0]
            speed_y[r, j] = expanded[1]
            spread[r, j] = expanded[2]
            source[r, j] = own_params[:, window] * expanded[3]

    def from_left(here, before):
        return jnp.where(first_lane, pltpu.roll(before, 1, 1), pltpu.roll(here, 1, 1))

    def from_right(here, after):
        return jnp.where(last_lane, pltpu.roll(after, LANES - 1, 1), pltpu.roll(here, LANES - 1, 1))

    def along_columns(t, r, k):
        start = k * per_chunk
        n = per_chunk
        at = (
            [lax.rem(start + tiles - 1, tiles)]
            + [start + i for i in range(n)]
            + [lax.rem(start + n, tiles)]
        )
        here = [cells[t, r, i] for i in at]
        turned = [pltpu.roll(c, LANES - 1, 1) for c in here]
        diffs = [
            (jnp.where(last_lane, turned[i + 1], turned[i]) if i <= n else turned[i]) - here[i]
            for i in range(n + 2)
        ]
        turned = [pltpu.roll(d, 1, 1) for d in diffs]
        earlier = [
            jnp.where(first_lane, turned[i - 1], turned[i]) if i > 0 else turned[i]
            for i in range(n + 2)
        ]
        halves = [half_minmod(earlier[i], diffs[i]) for i in range(n + 2)]
        upper = [here[i] + halves[i] for i in range(n + 1)]
        lower = [None] + [here[i] - halves[i] for i in range(1, n + 2)]
        upper_turned = [pltpu.roll(u, 1, 1) for u in upper]
        lower_turned = [None] + [pltpu.roll(v, LANES - 1, 1) for v in lower[1:]]
        for i in range(1, n + 1):
            forward = upper[i] - jnp.where(first_lane, upper_turned[i - 1], upper_turned[i])
            backward = jnp.where(last_lane, lower_turned[i + 1], lower_turned[i]) - lower[i]
            speed = speed_y[r, at[i]]
            change = jnp.where(speed > 0.0, forward, backward)
            partial_c[r, at[i]] = (
                here[i]
                - speed * change
                + spread[r, at[i]] * (diffs[i] - earlier[i])
                + source[r, at[i]]
            )

    def finish_rows(t, first, last, j, before, after, store):
        taken = before + [cells[t, r, j] for r in range(max(first - 2, 0), min(last + 2, rows))] + after
        new = across_rows(
            taken,
            [speed_x[r, j] for r in range(first, last)],
            [spread[r, j] for r in range(first, last)],
            [partial_c[r, j] for r in range(first, last)],
        )
        for r, value in zip(range(first, last), new):
            store(r, j, value)

    def one_step(t, final):
        def store(r, j, value):
            if final:
                final_c[r * tiles + j] = value
                field_v[pl.ds(of_tile(r, j), 8, stride=rows * tiles), :] = value
            else:
                cells[t + 1, r, j] = value

        @pl.loop(0, CHUNKS)
        def _(k):
            for r in (0, 1, rows - 2, rows - 1):
                along_columns(t, r, k)

        @pl.loop(0, CHUNKS)
        def _(k):
            wait_halo(t, 0, k)

            @pl.loop(0, per_chunk)
            def _(i):
                j = k * per_chunk + i
                finish_rows(t, 0, 2, j, [halo[t, 0, 0, j], halo[t, 0, 1, j]], [], store)

            if not final:
                send_halo(t + 1, 1, k)
            wait_halo(t, 1, k)

            @pl.loop(0, per_chunk)
            def _(i):
                j = k * per_chunk + i
                finish_rows(t, rows - 2, rows, j, [], [halo[t, 1, 0, j], halo[t, 1, 1, j]], store)

            if not final:
                send_halo(t + 1, 0, k)

            @pl.loop(2, rows - 2, step=2)
            def _(r):
                along_columns(t, r, k)
                along_columns(t, r + 1, k)

            @pl.loop(0, per_chunk)
            def _(i):
                finish_rows(t, 2, rows - 2, k * per_chunk + i, [], [], store)

    @pl.loop(0, STEPS - 1)
    def _(t):
        one_step(t, False)

    members = 32
    group_row = jnp.zeros((8, LANES), jnp.int32) - 1
    for m in range(members):
        group_row = jnp.where(lane == m, group_ref[m], group_row)
    slot_row = jnp.zeros((8, LANES), jnp.int32)
    for m in range(members):
        slot_row = slot_row + jnp.where((group_row == group_ref[m]) & (lane > m), 1, 0)
    sub = sublanes_of()
    group_own = jnp.zeros((8, LANES), jnp.int32)
    for i in range(8):
        group_own = jnp.where(sub == i, group_ref[ens * 8 + i], group_own)
    slot_own = jnp.zeros((8, LANES), jnp.int32)
    for m in range(members):
        slot_own = slot_own + jnp.where((group_own == group_ref[m]) & (sub + ens * 8 > m), 1, 0)
    in_slot = [jnp.where(slot_row == s, 1.0, 0.0) for s in range(4)]
    by_group = jnp.concatenate(
        [jnp.where(group_row == sub, in_slot[s], 0.0) for s in range(4)], axis=0
    )[:, :members]
    by_own = jnp.concatenate(
        [jnp.where(group_row == group_own, in_slot[s], 0.0) for s in range(4)], axis=0
    )[:, :members]

    def pick(chosen, held):
        return jnp.dot(chosen, held, precision=lax.Precision.HIGHEST, preferred_element_type=F32)

    spread_of = 1.0 / math.sqrt(3.0)

    def centred(four):
        mean = (four[0] + four[1] + four[2] + four[3]) * 0.25
        return [(x - mean) * spread_of for x in four]

    all_params[ens] = own_params[...]
    for p in range(1, 4):
        params_copy(p).wait_recv()
    columns = tiles * LANES
    piece = min(512, columns)

    @pl.loop(0, columns // piece)
    def _(c):
        window = pl.ds(pl.multiple_of(c * piece, piece), piece)
        held = jnp.concatenate([all_params[q, :, window] for q in range(4)], axis=0)
        ordered = pick(by_own, held)
        for s, value in enumerate(centred([ordered[s * 8 : s * 8 + 8] for s in range(4)])):
            moved[s, :, window] = value

    loads[3].wait()
    loads[4].wait()
    for p in range(1, 4):
        values_copy(p).wait_recv()
    ordered_values = pick(by_group, jnp.concatenate([all_values[q] for q in range(4)], axis=0))
    total_obs = float(obs_tiles * LANES * slabs)
    weights = [
        jnp.broadcast_to(1.0 / (variance_v[pl.ds(ens * quarter + i, 1), :] * total_obs), (8, LANES))
        for i in range(quarter)
    ]
    weight = jnp.concatenate(weights, axis=1)

    one_step(STEPS - 1, True)

    field_store = pltpu.make_async_copy(field_v, field_out, out_sem)
    field_store.start()

    def gather_quarter(q):
        @pl.loop(0, quarter)
        def _(i):
            tile = q * quarter + i

            def some(b, taken):
                for u in range(16):
                    at = b * 16 + u
                    where = index_ref[tile * LANES + at]
                    found = pltpu.roll(final_c[where >> 7], (at - where) & (LANES - 1), 1)
                    taken = jnp.where(lane == at, found, taken)
                return taken

            picked[tile] = lax.fori_loop(0, LANES // 16, some, jnp.zeros((8, LANES), F32))

    for p in range(1, 4):
        gather_quarter(lax.rem(ens + p, 4))
        picked_copy(p).start()
    gather_quarter(ens)
    for i in range(quarter):
        all_picked[ens, i] = picked[ens * quarter + i]
    for p in range(1, 4):
        picked_copy(p).wait_recv()

    held = jnp.concatenate(
        [
            jnp.concatenate([all_picked[q, i] for i in range(quarter)], axis=1)
            for q in range(4)
        ],
        axis=0,
    )
    ordered = pick(by_group, held)
    ordered = [ordered[s * 8 : s * 8 + 8] for s in range(4)]
    innovation = [
        (ordered_values[s * 8 : s * 8 + 8] - ordered[s]) * weight for s in range(4)
    ]
    anomalies = centred(ordered)
    weighted = [a * weight for a in anomalies]
    products = [(weighted[a], anomalies[b]) for a, b in PAIRS] + [
        (anomalies[a], innovation[b]) for a in range(4) for b in range(4)
    ]
    packed = jnp.zeros((8, LANES), F32)
    for position, (left, right) in enumerate(products):
        both = left * right
        folded = both[:, :LANES]
        for i in range(1, quarter):
            folded = folded + both[:, i * LANES : (i + 1) * LANES]
        packed = jnp.where(lane == position, jnp.sum(folded, axis=1, keepdims=True), packed)

    def sum_over(value, part, sums, me, count, device, send, recv):
        part[...] = value

        def copy(i, slot):
            return pltpu.make_async_remote_copy(
                src_ref=part,
                dst_ref=sums.at[me],
                send_sem=send.at[slot],
                recv_sem=recv.at[slot],
                device_id=device(i),
                device_id_type=MESH,
            )

        @pl.loop(1, count)
        def _(p):
            copy(lax.rem(me + p, count), p).start()

        sums[me] = value

        @pl.loop(1, count)
        def _(p):
            copy(lax.rem(me + p, count), p).wait()

        total = sums[0]
        for i in range(1, count):
            total = total + sums[i]
        return total

    total = sum_over(packed, part_near, sums_near, near_me, near_count, near_device, near_send, near_recv)
    total = sum_over(total, part_far, sums_far, far_me, far_count, far_device, far_send, far_recv)

    mine = jnp.zeros((8, LANES), F32)
    for g in range(GROUPS):
        mine = jnp.where(group_own == g, jnp.broadcast_to(total[g : g + 1], (8, LANES)), mine)

    def column(i):
        return jnp.broadcast_to(mine[:, i : i + 1], (8, LANES))

    a = {}
    for i, (p, q) in enumerate(PAIRS):
        a[p, q] = column(i) + (1.0 if p == q else 0.0)
    b = []
    for p in range(4):
        value = column(len(PAIRS) + p * 4)
        for q in range(1, 4):
            value = jnp.where(slot_own == q, column(len(PAIRS) + p * 4 + q), value)
        b.append(value)
    low = {}
    for p in range(4):
        for q in range(p + 1, 4):
            low[q, p] = a[p, q] / a[p, p]
        for q in range(p + 1, 4):
            for r in range(q, 4):
                a[q, r] = a[q, r] - low[q, p] * a[p, r]
    for p in range(4):
        for q in range(p + 1, 4):
            b[q] = b[q] - low[q, p] * b[p]
    solved = [b[p] / a[p, p] for p in range(4)]
    for p in range(2, -1, -1):
        for q in range(p + 1, 4):
            solved[p] = solved[p] - low[q, p] * solved[q]

    for j in range(tiles):
        window = pl.ds(j * LANES, LANES)
        value = own_params[:, window]
        for s in range(4):
            value = value + solved[s] * moved[s, :, window]
        params_out[:, window] = value

    for p in range(1, 4):
        params_copy(p).wait_send()
        values_copy(p).wait_send()
        picked_copy(p).wait_send()

    @pl.loop(0, STEPS)
    def _(t):
        @pl.loop(0, CHUNKS)
        def _(k):
            @pl.when(has_right)
            def _():
                halo_copy(t, 0, k).wait_send()

            @pl.when(has_left)
            def _():
                halo_copy(t, 1, k).wait_send()

    field_store.wait()


def local(tracer, coefficients, parameters, obs_index, obs_values, obs_variance, member_group):
    members, rows, columns = tracer.shape
    slabs = lax.axis_size("slab")
    tiles = columns // LANES
    obs_tiles = obs_index.shape[0] // LANES
    far_count = slabs // NEAR
    near_count = 4 * NEAR
    grid = (rows, tiles, 8, LANES)
    smem = pl.BlockSpec(memory_space=pltpu.SMEM)
    anywhere = pl.BlockSpec(memory_space=pl.ANY)
    vmem = pl.BlockSpec(memory_space=pltpu.VMEM)
    field, params = pl.pallas_call(
        functools.partial(kernel, slabs, tiles),
        out_shape=(
            jax.ShapeDtypeStruct((members * rows * tiles, LANES), F32),
            jax.ShapeDtypeStruct((members, columns), F32),
        ),
        in_specs=[smem, smem, anywhere, anywhere, anywhere, anywhere, anywhere],
        out_specs=(anywhere, vmem),
        scratch_shapes=[
            pltpu.VMEM((members * rows * tiles, LANES), F32),
            pltpu.VMEM((4, rows, columns), F32),
            pltpu.VMEM((members, columns), F32),
            pltpu.VMEM((obs_tiles, LANES), F32),
            pltpu.VMEM((STEPS,) + grid, F32),
            pltpu.VMEM((STEPS, 2, 2) + grid[1:], F32),
            pltpu.VMEM(grid, F32),
            pltpu.VMEM(grid, F32),
            pltpu.VMEM(grid, F32),
            pltpu.VMEM(grid, F32),
            pltpu.VMEM(grid, F32),
            pltpu.VMEM((rows * tiles, 8, LANES), F32),
            pltpu.VMEM((members * rows * tiles, LANES), F32),
            pltpu.VMEM((4, members, columns), F32),
            pltpu.VMEM((4, members, obs_tiles // 4 * LANES), F32),
            pltpu.VMEM((obs_tiles, 8, LANES), F32),
            pltpu.VMEM((4, obs_tiles // 4, 8, LANES), F32),
            pltpu.VMEM((4, members, columns), F32),
            pltpu.VMEM((8, LANES), F32),
            pltpu.VMEM((8, LANES), F32),
            pltpu.VMEM((near_count, 8, LANES), F32),
            pltpu.VMEM((far_count, 8, LANES), F32),
            pltpu.SemaphoreType.DMA((5,)),
            pltpu.SemaphoreType.DMA,
            pltpu.SemaphoreType.DMA((STEPS, 2, CHUNKS)),
            pltpu.SemaphoreType.DMA((STEPS, 2, CHUNKS)),
            pltpu.SemaphoreType.DMA((3, 4)),
            pltpu.SemaphoreType.DMA((3, 4)),
            pltpu.SemaphoreType.DMA((near_count,)),
            pltpu.SemaphoreType.DMA((near_count,)),
            pltpu.SemaphoreType.DMA((far_count,)),
            pltpu.SemaphoreType.DMA((far_count,)),
        ],
        compiler_params=pltpu.CompilerParams(
            collective_id=0, has_side_effects=True, vmem_limit_bytes=56 * 1024 * 1024
        ),
    )(
        member_group,
        obs_index,
        tracer.reshape(members, rows // 8, 8, tiles, LANES).transpose(0, 1, 3, 2, 4).reshape(-1, LANES),
        coefficients,
        parameters,
        obs_values,
        obs_variance.reshape(obs_tiles, LANES),
    )
    field = field.reshape(members, rows // 8, tiles, 8, LANES).transpose(0, 1, 3, 2, 4)
    return field.reshape(members, rows, columns), params


def solution(mesh):
    in_specs = (
        P("ens", "slab", None),
        P(None, "slab", None),
        P("ens", None),
        P("slab"),
        P("ens", "slab"),
        P("slab"),
        P(),
    )
    out_specs = (P("ens", "slab", None), P("ens", None))
    return jax.shard_map(local, mesh=mesh, in_specs=in_specs, out_specs=out_specs, check_vma=False)
```

time: 535 us -> 87.5 us (0.16)
  the two profiles are of different devices: /device:TPU:24 before, /device:TPU:1 now
where the time goes in v1:
time: 87.5 us; the launch traced here: 87.3 us
  Pallas kernels  82.9 us (95%)
  local copies, waits for them, and re-layouts  3.81 us (4%)
    pallas_call x1, Pallas kernels, local(): pl.pallas_call(functools.partial(kernel, slabs, tiles), out_shape=(jax.Sh...  82.9 us
    unnamed x4, local copies, waits for them, and re-layouts  3.81 us

profile of v1, /device:TPU:1, one launch (start us, length us, event | category | flops | bytes accessed | tf_op | source)
XLA Modules:
  0.0 87.3 jit_solution(11452516285934838305)
XLA Ops:
  0.6 82.9 %shard_map.86 = (f32[4096,128]{1,0:T(8,128)}, f32[8,4096]{1,0:T(8,128)}) custom-call(s32[32]{0:T(128)} %group_ref.1, s32[2048]{0:T(1024)} %index_ref.1, f32[4096,128]{1,0:T(8,128)} %bitcast.11, f32[4,16,4096]{2,1,0:T(8,128)} %coef_ref.1, f32[8,4096]{1,0:T(8,128)} %params_ref.1, f32[8,2048]{1,0:T(8,128)} %values_ref.1, f32[16,128]{1,0:T(8,128)} %bitcast.13), custom_call_target="tpu_custom_call" | custom-call | tf_op jit(solution)/shard_map/pallas_call | solution.py:571
  83.5 0.0 copy-start
  83.5 3.1 %copy.11 = f32[8,16,4096]{2,1,0:T(8,128)} copy(f32[8,16,4096]{2,1,0:T(8,128)} %bitcast.12) | data formatting | bytes 4194304
  86.7 0.0 copy-done
  86.7 0.7 copy.12
Async XLA Ops:
  83.5 3.2 %copy-start = (f32[8,4096]{1,0:T(8,128)S(1)}, f32[8,4096]{1,0:T(8,128)}, u32[]{:S(2)}) copy-start(f32[8,4096]{1,0:T(8,128)} %get-tuple-element.9) | copy-start | bytes 393220

commit v2 on v1

--- a/solution.py
+++ b/solution.py
@@ -13,6 +13,8 @@
 LANES = 128
 CHUNKS = 4
 NEAR = 4
+BLOCKS = 16
+EDGE = 8
 MESH = pl.DeviceIdType.MESH
 F32 = jnp.float32
 PAIRS = [(a, b) for a in range(4) for b in range(a, 4)]
@@ -24,6 +26,14 @@
 
 def sublanes_of():
     return lax.broadcasted_iota(jnp.int32, (8, LANES), 0)
+
+
+def parts_of(value):
+    high = value.astype(jnp.bfloat16)
+    rest = value - high.astype(F32)
+    middle = rest.astype(jnp.bfloat16)
+    low = (rest - middle.astype(F32)).astype(jnp.bfloat16)
+    return jnp.concatenate([high, middle, low], axis=1)
 
 
 def half_minmod(left, right):
@@ -60,14 +70,20 @@
     coef_v,
     own_params,
     variance_v,
+    index_v,
+    place_v,
+    place,
+    spread_out,
+    pick_out,
+    params_t,
+    coef_x,
     cells,
     halo,
-    speed_x,
-    speed_y,
-    spread,
-    source,
+    slopes,
     partial_c,
     final_c,
+    mask_v,
+    found,
     field_v,
     all_params,
     all_values,
@@ -92,18 +108,20 @@
     ens = lax.axis_index("ens")
     slab = lax.axis_index("slab")
     rows = 16
-    per_chunk = tiles // CHUNKS
+    segment = tiles * LANES // BLOCKS
+    halves = segment // LANES
+    per_chunk = segment // CHUNKS
+    groups = per_chunk // 8
     far_count = slabs // NEAR
     near_count = 4 * NEAR
-    obs_tiles = picked.shape[0]
-    quarter = obs_tiles // 4
+    quarter = picked.shape[1]
+    obs_tiles = 4 * quarter
     has_left = slab > 0
     has_right = slab < slabs - 1
     near_me = ens * NEAR + lax.rem(slab, NEAR)
     far_me = slab // NEAR
     lane = lanes_of()
-    first_lane = lane == 0
-    last_lane = lane == LANES - 1
+    sub = sublanes_of()
 
     def near_device(i):
         return (i // NEAR, far_me * NEAR + lax.rem(i, NEAR))
@@ -121,6 +139,7 @@
             all_values.at[ens],
             load_sem.at[4],
         ),
+        pltpu.make_async_copy(index_ref, index_v, load_sem.at[5]),
     ]
     for load in loads:
         load.start()
@@ -150,16 +169,22 @@
     loads[0].wait()
 
     def of_tile(row, j):
-        return (row // 8 * tiles + j) * 8 + row % 8
+        return (row // 8 * tiles + j) * 8 + lax.rem(row, 8)
 
     def take_row(row):
-        for j in range(tiles):
-            cells[0, row, j] = tracer_v[pl.ds(of_tile(row, j), 8, stride=rows * tiles), :]
-
-    take_row(0)
-    take_row(1)
-    take_row(rows - 2)
-    take_row(rows - 1)
+        for h in range(halves):
+            block = [
+                tracer_v[pl.ds(of_tile(row, b * halves + h), 8, stride=rows * tiles), :]
+                for b in range(BLOCKS)
+            ]
+            cells[0, row, pl.ds(EDGE + h * LANES, LANES), :] = jnp.transpose(jnp.concatenate(block, axis=0))
+
+    def edge_row(i):
+        return i + i // 2 * (rows - 4)
+
+    @pl.loop(0, 4)
+    def _(i):
+        take_row(edge_row(i))
 
     zero = jnp.zeros((8, LANES), F32)
 
@@ -167,8 +192,8 @@
         @pl.loop(0, STEPS)
         def _(t):
             for r in range(2):
-                for j in range(tiles):
-                    halo[t, side, r, j] = zero
+                for i in range(segment // 8):
+                    halo[t, side, r, pl.ds(i * 8, 8), :] = zero
 
     pl.when(jnp.logical_not(has_left))(functools.partial(clear, 0))
     pl.when(jnp.logical_not(has_right))(functools.partial(clear, 1))
@@ -177,10 +202,14 @@
     pl.semaphore_wait(barrier, near_count + far_count - 2 + neighbours)
 
     def halo_copy(t, side, k):
-        window = pl.ds(k * per_chunk, per_chunk)
+        start = pl.multiple_of(k * per_chunk, per_chunk)
         return pltpu.make_async_remote_copy(
-            src_ref=cells.at[t, pl.ds(rows - 2, 2) if side == 0 else pl.ds(0, 2), window],
-            dst_ref=halo.at[t, side, :, window],
+            src_ref=cells.at[
+                t,
+                pl.ds(rows - 2, 2) if side == 0 else pl.ds(0, 2),
+                pl.ds(pl.multiple_of(EDGE + start, 8), per_chunk),
+            ],
+            dst_ref=halo.at[t, side, :, pl.ds(start, per_chunk)],
             send_sem=halo_send.at[t, side, k],
             recv_sem=halo_recv.at[t, side, k],
             device_id=(ens, slab + 1 if side == 0 else slab - 1),
@@ -228,7 +257,7 @@
     def picked_copy(p):
         target = lax.rem(ens + p, 4)
         return pltpu.make_async_remote_copy(
-            src_ref=picked.at[pl.ds(target * quarter, quarter)],
+            src_ref=picked.at[target],
             dst_ref=all_picked.at[ens],
             send_sem=ens_send.at[2, p],
             recv_sem=ens_recv.at[2, p],
@@ -240,118 +269,134 @@
         params_copy(p).start()
         values_copy(p).start()
 
-    for row in range(2, rows - 2):
+    from_lane = lax.broadcasted_iota(jnp.int32, (3 * LANES, LANES), 0)
+    to_lane = lax.broadcasted_iota(jnp.int32, (3 * LANES, LANES), 1)
+    same_block = ((from_lane >> 3) & (BLOCKS - 1)) == (to_lane >> 3)
+    for r in range(8):
+        spread_out[:, pl.ds(r * LANES, LANES)] = jnp.where(
+            same_block & ((from_lane & 7) == r), 1.0, 0.0
+        ).astype(jnp.bfloat16)
+    for i in range(quarter):
+        pick_out[i] = jnp.where(
+            ((from_lane & 7) == (to_lane & 7)) & ((to_lane >> 3) == i), 1.0, 0.0
+        ).astype(jnp.bfloat16)
+
+    @pl.loop(2, rows - 2)
+    def _(row):
         take_row(row)
 
+    for h in range(halves):
+        block = [own_params[:, pl.ds((b * halves + h) * LANES, LANES)] for b in range(BLOCKS)]
+        params_t[pl.ds(h * LANES, LANES), :] = jnp.transpose(jnp.concatenate(block, axis=0))
+
     loads[1].wait()
 
-    @pl.loop(0, tiles)
-    def _(j):
-        window = pl.ds(pl.multiple_of(j * LANES, LANES), LANES)
-        for r in range(rows):
-            expanded = [
-                jnp.broadcast_to(coef_v[c, pl.ds(r, 1), window], (8, LANES)) for c in range(4)
-            ]
-            speed_x[r, j] = expanded[0]
-            speed_y[r, j] = expanded[1]
-            spread[r, j] = expanded[2]
-            source[r, j] = own_params[:, window] * expanded[3]
-
-    def from_left(here, before):
-        return jnp.where(first_lane, pltpu.roll(before, 1, 1), pltpu.roll(here, 1, 1))
-
-    def from_right(here, after):
-        return jnp.where(last_lane, pltpu.roll(after, LANES - 1, 1), pltpu.roll(here, LANES - 1, 1))
-
-    def along_columns(t, r, k):
+    def expand(c, eight, h, scale):
+        block = [coef_v[(c * 2 + eight) * tiles + b * halves + h] for b in range(BLOCKS)]
+        turned = jnp.transpose(jnp.concatenate(block, axis=0))
+        wide = jnp.dot(parts_of(turned), spread_out[...], preferred_element_type=F32)
+        window = pl.ds(pl.multiple_of(h * LANES, LANES), LANES)
+        for r in range(8):
+            value = wide[:, r * LANES : (r + 1) * LANES]
+            if scale:
+                value = value * params_t[window, :]
+            coef_x[c, eight * 8 + r, window, :] = value
+
+    @pl.loop(0, 3 * 2 * halves)
+    def _(n):
+        expand(n // (2 * halves), lax.rem(n // halves, 2), lax.rem(n, halves), False)
+
+    @pl.loop(0, 2 * halves)
+    def _(n):
+        expand(3, n // halves, lax.rem(n, halves), True)
+
+    def wrap_row(t, r):
+        cells[t, r, pl.ds(0, 8), :] = pltpu.roll(cells[t, r, pl.ds(EDGE + segment - 8, 8), :], 8, 1)
+        cells[t, r, pl.ds(EDGE + segment, 8), :] = pltpu.roll(cells[t, r, pl.ds(EDGE, 8), :], LANES - 8, 1)
+
+    def along_columns(t, rows_here, k):
         start = k * per_chunk
-        n = per_chunk
-        at = (
-            [lax.rem(start + tiles - 1, tiles)]
-            + [start + i for i in range(n)]
-            + [lax.rem(start + n, tiles)]
-        )
-        here = [cells[t, r, i] for i in at]
-        turned = [pltpu.roll(c, LANES - 1, 1) for c in here]
-        diffs = [
-            (jnp.where(last_lane, turned[i + 1], turned[i]) if i <= n else turned[i]) - here[i]
-            for i in range(n + 2)
-        ]
-        turned = [pltpu.roll(d, 1, 1) for d in diffs]
-        earlier = [
-            jnp.where(first_lane, turned[i - 1], turned[i]) if i > 0 else turned[i]
-            for i in range(n + 2)
-        ]
-        halves = [half_minmod(earlier[i], diffs[i]) for i in range(n + 2)]
-        upper = [here[i] + halves[i] for i in range(n + 1)]
-        lower = [None] + [here[i] - halves[i] for i in range(1, n + 2)]
-        upper_turned = [pltpu.roll(u, 1, 1) for u in upper]
-        lower_turned = [None] + [pltpu.roll(v, LANES - 1, 1) for v in lower[1:]]
-        for i in range(1, n + 1):
-            forward = upper[i] - jnp.where(first_lane, upper_turned[i - 1], upper_turned[i])
-            backward = jnp.where(last_lane, lower_turned[i + 1], lower_turned[i]) - lower[i]
-            speed = speed_y[r, at[i]]
-            change = jnp.where(speed > 0.0, forward, backward)
-            partial_c[r, at[i]] = (
-                here[i]
-                - speed * change
-                + spread[r, at[i]] * (diffs[i] - earlier[i])
-                + source[r, at[i]]
-            )
-
-    def finish_rows(t, first, last, j, before, after, store):
-        taken = before + [cells[t, r, j] for r in range(max(first - 2, 0), min(last + 2, rows))] + after
+        for s, r in enumerate(rows_here):
+            for i in range(groups + 1):
+                at = start + (EDGE - 1 + i * 8)
+                before, here, after = [cells[t, r, pl.ds(at + d, 8), :] for d in (-1, 0, 1)]
+                slopes[s, pl.ds(i * 8, 8), :] = half_minmod(here - before, after - here)
+        for s, r in enumerate(rows_here):
+            for i in range(groups):
+                at = start + (EDGE + i * 8)
+                window = pl.ds(pl.multiple_of(start + i * 8, 8), 8)
+                before, here, after = [cells[t, r, pl.ds(at + d, 8), :] for d in (-1, 0, 1)]
+                half_before, half, half_after = [slopes[s, pl.ds(i * 8 + d, 8), :] for d in (0, 1, 2)]
+                forward = (here + half) - (before + half_before)
+                backward = (after - half_after) - (here - half)
+                speed = coef_x[1, r, window, :]
+                partial_c[r, window, :] = (
+                    here
+                    - speed * jnp.where(speed > 0.0, forward, backward)
+                    + coef_x[2, r, window, :] * ((after - here) - (here - before))
+                    + coef_x[3, r, window, :]
+                )
+
+    def finish_rows(t, first, last, i, before, after, store):
+        window = pl.ds(pl.multiple_of(i * 8, 8), 8)
+        inner = pl.ds(pl.multiple_of(EDGE + i * 8, 8), 8)
+        taken = (
+            [halo[t, 0, r, window, :] for r in range(before)]
+            + [cells[t, r, inner, :] for r in range(max(first - 2, 0), min(last + 2, rows))]
+            + [halo[t, 1, r, window, :] for r in range(after)]
+        )
         new = across_rows(
             taken,
-            [speed_x[r, j] for r in range(first, last)],
-            [spread[r, j] for r in range(first, last)],
-            [partial_c[r, j] for r in range(first, last)],
+            [coef_x[0, r, window, :] for r in range(first, last)],
+            [coef_x[2, r, window, :] for r in range(first, last)],
+            [partial_c[r, window, :] for r in range(first, last)],
         )
         for r, value in zip(range(first, last), new):
-            store(r, j, value)
+            store(r, i, value)
 
     def one_step(t, final):
-        def store(r, j, value):
+        def store(r, i, value):
             if final:
-                final_c[r * tiles + j] = value
-                field_v[pl.ds(of_tile(r, j), 8, stride=rows * tiles), :] = value
+                final_c[pl.ds(pl.multiple_of(r * segment + i * 8, 8), 8), :] = value
             else:
-                cells[t + 1, r, j] = value
+                cells[t + 1, r, pl.ds(pl.multiple_of(EDGE + i * 8, 8), 8), :] = value
+
+        for r in range(rows):
+            wrap_row(t, r)
 
         @pl.loop(0, CHUNKS)
         def _(k):
-            for r in (0, 1, rows - 2, rows - 1):
-                along_columns(t, r, k)
+            along_columns(t, (0, 1), k)
+            along_columns(t, (rows - 2, rows - 1), k)
 
         @pl.loop(0, CHUNKS)
         def _(k):
             wait_halo(t, 0, k)
 
-            @pl.loop(0, per_chunk)
+            @pl.loop(0, groups, step=2)
             def _(i):
-                j = k * per_chunk + i
-                finish_rows(t, 0, 2, j, [halo[t, 0, 0, j], halo[t, 0, 1, j]], [], store)
+                for u in range(2):
+                    finish_rows(t, 0, 2, k * groups + i + u, 2, 0, store)
 
             if not final:
                 send_halo(t + 1, 1, k)
             wait_halo(t, 1, k)
 
-            @pl.loop(0, per_chunk)
+            @pl.loop(0, groups, step=2)
             def _(i):
-                j = k * per_chunk + i
-                finish_rows(t, rows - 2, rows, j, [], [halo[t, 1, 0, j], halo[t, 1, 1, j]], store)
+                for u in range(2):
+                    finish_rows(t, rows - 2, rows, k * groups + i + u, 0, 2, store)
 
             if not final:
                 send_halo(t + 1, 0, k)
 
             @pl.loop(2, rows - 2, step=2)
             def _(r):
-                along_columns(t, r, k)
-                along_columns(t, r + 1, k)
-
-            @pl.loop(0, per_chunk)
+                along_columns(t, (r, r + 1), k)
+
+            @pl.loop(0, groups)
             def _(i):
-                finish_rows(t, 2, rows - 2, k * per_chunk + i, [], [], store)
+                finish_rows(t, 2, rows - 2, k * groups + i, 0, 0, store)
 
     @pl.loop(0, STEPS - 1)
     def _(t):
@@ -364,7 +409,6 @@
     slot_row = jnp.zeros((8, LANES), jnp.int32)
     for m in range(members):
         slot_row = slot_row + jnp.where((group_row == group_ref[m]) & (lane > m), 1, 0)
-    sub = sublanes_of()
     group_own = jnp.zeros((8, LANES), jnp.int32)
     for i in range(8):
         group_own = jnp.where(sub == i, group_ref[ens * 8 + i], group_own)
@@ -414,32 +458,61 @@
     ]
     weight = jnp.concatenate(weights, axis=1)
 
+    loads[5].wait()
+    cell = index_v[...]
+    column_of = cell & (tiles * LANES - 1)
+    place_v[...] = cell // (tiles * LANES) * segment + (column_of & (segment - 1))
+    to_smem = pltpu.make_async_copy(place_v, place, load_sem.at[6])
+    to_smem.start()
+    block_of = jnp.transpose((column_of // segment).astype(F32))
+    lane_block = (lax.broadcasted_iota(jnp.int32, (LANES, LANES), 1) >> 3).astype(F32)
+    for i in range(obs_tiles):
+        mask_v[i] = jnp.where(
+            jnp.broadcast_to(block_of[:, i : i + 1], (LANES, LANES)) == lane_block, 1.0, 0.0
+        )
+    to_smem.wait()
+
     one_step(STEPS - 1, True)
 
-    field_store = pltpu.make_async_copy(field_v, field_out, out_sem)
-    field_store.start()
-
     def gather_quarter(q):
-        @pl.loop(0, quarter)
-        def _(i):
+        def one_tile(i, total):
             tile = q * quarter + i
 
-            def some(b, taken):
-                for u in range(16):
-                    at = b * 16 + u
-                    where = index_ref[tile * LANES + at]
-                    found = pltpu.roll(final_c[where >> 7], (at - where) & (LANES - 1), 1)
-                    taken = jnp.where(lane == at, found, taken)
-                return taken
-
-            picked[tile] = lax.fori_loop(0, LANES // 16, some, jnp.zeros((8, LANES), F32))
+            @pl.loop(0, LANES // 32)
+            def _(g):
+                for v in range(4):
+                    taken = jnp.zeros((8, LANES), F32)
+                    for u in range(8):
+                        row = final_c[pl.ds(place[tile, g * 32 + v * 8 + u], 1), :]
+                        taken = jnp.where(sub == u, jnp.broadcast_to(row, (8, LANES)), taken)
+                    window = pl.ds(pl.multiple_of(g * 32 + v * 8, 8), 8)
+                    found[window, :] = taken * mask_v[tile, window, :]
+
+            return total + jnp.dot(parts_of(found[...]), pick_out[i], preferred_element_type=F32)
+
+        total = lax.fori_loop(0, quarter, one_tile, jnp.zeros((LANES, LANES), F32))
+        turned = jnp.transpose(total)
+        for i in range(quarter):
+            picked[q, i] = turned[i * 8 : i * 8 + 8]
+
+    def emit_rows(first, last):
+        @pl.loop(first, last)
+        def _(r):
+            for h in range(halves):
+                start = pl.multiple_of(r * segment + h * LANES, LANES)
+                turned = jnp.transpose(final_c[pl.ds(start, LANES), :])
+                for b in range(BLOCKS):
+                    field_v[pl.ds(of_tile(r, b * halves + h), 8, stride=rows * tiles), :] = turned[
+                        b * 8 : b * 8 + 8
+                    ]
 
     for p in range(1, 4):
         gather_quarter(lax.rem(ens + p, 4))
         picked_copy(p).start()
     gather_quarter(ens)
     for i in range(quarter):
-        all_picked[ens, i] = picked[ens * quarter + i]
+        all_picked[ens, i] = picked[ens, i]
+    emit_rows(0, 6)
     for p in range(1, 4):
         picked_copy(p).wait_recv()
 
@@ -468,7 +541,7 @@
             folded = folded + both[:, i * LANES : (i + 1) * LANES]
         packed = jnp.where(lane == position, jnp.sum(folded, axis=1, keepdims=True), packed)
 
-    def sum_over(value, part, sums, me, count, device, send, recv):
+    def sum_over(value, part, sums, me, count, device, send, recv, meanwhile):
         part[...] = value
 
         def copy(i, slot):
@@ -486,6 +559,7 @@
             copy(lax.rem(me + p, count), p).start()
 
         sums[me] = value
+        meanwhile()
 
         @pl.loop(1, count)
         def _(p):
@@ -496,8 +570,26 @@
             total = total + sums[i]
         return total
 
-    total = sum_over(packed, part_near, sums_near, near_me, near_count, near_device, near_send, near_recv)
-    total = sum_over(total, part_far, sums_far, far_me, far_count, far_device, far_send, far_recv)
+    field_store = pltpu.make_async_copy(field_v, field_out, out_sem)
+
+    def rest_of_field():
+        emit_rows(11, rows)
+        field_store.start()
+
+    total = sum_over(
+        packed,
+        part_near,
+        sums_near,
+        near_me,
+        near_count,
+        near_device,
+        near_send,
+        near_recv,
+        lambda: emit_rows(6, 11),
+    )
+    total = sum_over(
+        total, part_far, sums_far, far_me, far_count, far_device, far_send, far_recv, rest_of_field
+    )
 
     mine = jnp.zeros((8, LANES), F32)
     for g in range(GROUPS):
@@ -564,7 +656,8 @@
     obs_tiles = obs_index.shape[0] // LANES
     far_count = slabs // NEAR
     near_count = 4 * NEAR
-    grid = (rows, tiles, 8, LANES)
+    segment = columns // BLOCKS
+    wide = (rows, segment, LANES)
     smem = pl.BlockSpec(memory_space=pltpu.SMEM)
     anywhere = pl.BlockSpec(memory_space=pl.ANY)
     vmem = pl.BlockSpec(memory_space=pltpu.VMEM)
@@ -574,32 +667,38 @@
             jax.ShapeDtypeStruct((members * rows * tiles, LANES), F32),
             jax.ShapeDtypeStruct((members, columns), F32),
         ),
-        in_specs=[smem, smem, anywhere, anywhere, anywhere, anywhere, anywhere],
+        in_specs=[smem, anywhere, anywhere, anywhere, anywhere, anywhere, anywhere],
         out_specs=(anywhere, vmem),
         scratch_shapes=[
             pltpu.VMEM((members * rows * tiles, LANES), F32),
-            pltpu.VMEM((4, rows, columns), F32),
+            pltpu.VMEM((4 * rows // 8 * tiles, 8, LANES), F32),
             pltpu.VMEM((members, columns), F32),
             pltpu.VMEM((obs_tiles, LANES), F32),
-            pltpu.VMEM((STEPS,) + grid, F32),
-            pltpu.VMEM((STEPS, 2, 2) + grid[1:], F32),
-            pltpu.VMEM(grid, F32),
-            pltpu.VMEM(grid, F32),
-            pltpu.VMEM(grid, F32),
-            pltpu.VMEM(grid, F32),
-            pltpu.VMEM(grid, F32),
-            pltpu.VMEM((rows * tiles, 8, LANES), F32),
+            pltpu.VMEM((obs_tiles, LANES), jnp.int32),
+            pltpu.VMEM((obs_tiles, LANES), jnp.int32),
+            pltpu.SMEM((obs_tiles, LANES), jnp.int32),
+            pltpu.VMEM((3 * LANES, 8 * LANES), jnp.bfloat16),
+            pltpu.VMEM((obs_tiles // 4, 3 * LANES, LANES), jnp.bfloat16),
+            pltpu.VMEM((segment, LANES), F32),
+            pltpu.VMEM((4,) + wide, F32),
+            pltpu.VMEM((STEPS, rows, segment + 2 * EDGE, LANES), F32),
+            pltpu.VMEM((STEPS, 2, 2, segment, LANES), F32),
+            pltpu.VMEM((2, segment // CHUNKS + 8, LANES), F32),
+            pltpu.VMEM(wide, F32),
+            pltpu.VMEM((rows * segment, LANES), F32),
+            pltpu.VMEM((obs_tiles, LANES, LANES), F32),
+            pltpu.VMEM((LANES, LANES), F32),
             pltpu.VMEM((members * rows * tiles, LANES), F32),
             pltpu.VMEM((4, members, columns), F32),
             pltpu.VMEM((4, members, obs_tiles // 4 * LANES), F32),
-            pltpu.VMEM((obs_tiles, 8, LANES), F32),
+            pltpu.VMEM((4, obs_tiles // 4, 8, LANES), F32),
             pltpu.VMEM((4, obs_tiles // 4, 8, LANES), F32),
             pltpu.VMEM((4, members, columns), F32),
             pltpu.VMEM((8, LANES), F32),
             pltpu.VMEM((8, LANES), F32),
             pltpu.VMEM((near_count, 8, LANES), F32),
             pltpu.VMEM((far_count, 8, LANES), F32),
-            pltpu.SemaphoreType.DMA((5,)),
+            pltpu.SemaphoreType.DMA((7,)),
             pltpu.SemaphoreType.DMA,
             pltpu.SemaphoreType.DMA((STEPS, 2, CHUNKS)),
             pltpu.SemaphoreType.DMA((STEPS, 2, CHUNKS)),
@@ -615,9 +714,9 @@
         ),
     )(
         member_group,
-        obs_index,
+        obs_index.reshape(obs_tiles, LANES),
         tracer.reshape(members, rows // 8, 8, tiles, LANES).transpose(0, 1, 3, 2, 4).reshape(-1, LANES),
-        coefficients,
+        coefficients.reshape(4, rows // 8, 8, tiles, LANES).transpose(0, 1, 3, 2, 4).reshape(-1, 8, LANES),
         parameters,
         obs_values,
         obs_variance.reshape(obs_tiles, LANES),

time: 87.5 us -> 72 us (0.82)
  Pallas kernels: 82.9 us -> 67.4 us
    pallas_call x1, Pallas kernels: 82.9 us -> 67.4 us  [local(): pl.pallas_call(functools.partial(kernel, slabs, tiles), out_shape=(jax.Sh...]
where the time goes in v2:
time: 72 us; the launch traced here: 71.9 us
  Pallas kernels  67.4 us (94%)
  local copies, waits for them, and re-layouts  3.81 us (5%)
    pallas_call x1, Pallas kernels, local(): pl.pallas_call(functools.partial(kernel, slabs, tiles), out_shape=(jax.Sh...  67.4 us
    unnamed x4, local copies, waits for them, and re-layouts  3.81 us

profile of v2, /device:TPU:1, one launch (start us, length us, event | category | flops | bytes accessed | tf_op | source)
XLA Modules:
  0.0 71.9 jit_solution(2534678682734357379)
XLA Ops:
  0.6 67.4 %shard_map.86 = (f32[4096,128]{1,0:T(8,128)}, f32[8,4096]{1,0:T(8,128)}) custom-call(s32[32]{0:T(128)} %group_ref.1, s32[16,128]{1,0:T(8,128)} %bitcast.20, f32[4096,128]{1,0:T(8,128)} %bitcast.17, f32[256,8,128]{2,1,0:T(8,128)} %bitcast.19, f32[8,4096]{1,0:T(8,128)} %params_ref.1, f32[8,2048]{1,0:T(8,128)} %values_ref.1, f32[16,128]{1,0:T(8,128)} %bitcast.21), custom_call_target="tpu_custom_call" | custom-call | tf_op jit(solution)/shard_map/pallas_call | solution.py:664
  68.0 0.0 copy-start
  68.1 3.1 %copy.11 = f32[8,16,4096]{2,1,0:T(8,128)} copy(f32[8,16,4096]{2,1,0:T(8,128)} %bitcast.18) | data formatting | bytes 4194304
  71.2 0.0 copy-done
  71.2 0.7 copy.12
Async XLA Ops:
  68.0 3.2 %copy-start = (f32[8,4096]{1,0:T(8,128)S(1)}, f32[8,4096]{1,0:T(8,128)}, u32[]{:S(2)}) copy-start(f32[8,4096]{1,0:T(8,128)} %get-tuple-element.9) | copy-start | bytes 393220

commit v3 on v2

--- a/solution.py
+++ b/solution.py
@@ -11,7 +11,7 @@
 STEPS = 4
 GROUPS = 8
 LANES = 128
-CHUNKS = 4
+CHUNKS = 2
 NEAR = 4
 BLOCKS = 16
 EDGE = 8
@@ -44,12 +44,11 @@
     count = len(rows) - 4
     diffs = [rows[i + 1] - rows[i] for i in range(count + 3)]
     halves = [half_minmod(diffs[i], diffs[i + 1]) for i in range(count + 2)]
-    upper = [rows[i + 1] + halves[i] for i in range(count + 2)]
-    lower = [rows[i + 1] - halves[i] for i in range(count + 2)]
+    bends = [halves[i + 1] - halves[i] for i in range(count + 1)]
     out = []
     for i in range(count):
         speed = speeds[i]
-        change = jnp.where(speed > 0.0, upper[i + 1] - upper[i], lower[i + 2] - lower[i + 1])
+        change = jnp.where(speed > 0.0, diffs[i + 1] + bends[i], diffs[i + 2] - bends[i + 1])
         out.append(bases[i] - speed * change + spreads[i] * (diffs[i + 2] - diffs[i + 1]))
     return out
 
@@ -277,7 +276,7 @@
             same_block & ((from_lane & 7) == r), 1.0, 0.0
         ).astype(jnp.bfloat16)
     for i in range(quarter):
-        pick_out[i] = jnp.where(
+        pick_out[pl.ds(i * 3 * LANES, 3 * LANES), :] = jnp.where(
             ((from_lane & 7) == (to_lane & 7)) & ((to_lane >> 3) == i), 1.0, 0.0
         ).astype(jnp.bfloat16)
 
@@ -327,13 +326,14 @@
                 window = pl.ds(pl.multiple_of(start + i * 8, 8), 8)
                 before, here, after = [cells[t, r, pl.ds(at + d, 8), :] for d in (-1, 0, 1)]
                 half_before, half, half_after = [slopes[s, pl.ds(i * 8 + d, 8), :] for d in (0, 1, 2)]
-                forward = (here + half) - (before + half_before)
-                backward = (after - half_after) - (here - half)
+                down, up = here - before, after - here
+                forward = down + (half - half_before)
+                backward = up - (half_after - half)
                 speed = coef_x[1, r, window, :]
                 partial_c[r, window, :] = (
                     here
                     - speed * jnp.where(speed > 0.0, forward, backward)
-                    + coef_x[2, r, window, :] * ((after - here) - (here - before))
+                    + coef_x[2, r, window, :] * (up - down)
                     + coef_x[3, r, window, :]
                 )
 
@@ -364,32 +364,24 @@
         for r in range(rows):
             wrap_row(t, r)
 
-        @pl.loop(0, CHUNKS)
-        def _(k):
+        def edges(k):
             along_columns(t, (0, 1), k)
             along_columns(t, (rows - 2, rows - 1), k)
-
-        @pl.loop(0, CHUNKS)
-        def _(k):
-            wait_halo(t, 0, k)
-
-            @pl.loop(0, groups, step=2)
-            def _(i):
-                for u in range(2):
-                    finish_rows(t, 0, 2, k * groups + i + u, 2, 0, store)
-
-            if not final:
-                send_halo(t + 1, 1, k)
-            wait_halo(t, 1, k)
-
-            @pl.loop(0, groups, step=2)
-            def _(i):
-                for u in range(2):
-                    finish_rows(t, rows - 2, rows, k * groups + i + u, 0, 2, store)
-
-            if not final:
-                send_halo(t + 1, 0, k)
-
+            for side in range(2):
+                wait_halo(t, side, k)
+                first = (rows - 2) * side
+
+                @pl.loop(0, groups, step=4)
+                def _(i):
+                    for u in range(4):
+                        finish_rows(
+                            t, first, first + 2, k * groups + i + u, 2 - 2 * side, 2 * side, store
+                        )
+
+                if not final:
+                    send_halo(t + 1, 1 - side, k)
+
+        def inside(k):
             @pl.loop(2, rows - 2, step=2)
             def _(r):
                 along_columns(t, (r, r + 1), k)
@@ -397,6 +389,12 @@
             @pl.loop(0, groups)
             def _(i):
                 finish_rows(t, 2, rows - 2, k * groups + i, 0, 0, store)
+
+        @pl.loop(0, CHUNKS)
+        def _(k):
+            pl.when(k == CHUNKS - 1)(lambda: inside(k))
+            edges(k)
+            pl.when(k < CHUNKS - 1)(lambda: inside(k))
 
     @pl.loop(0, STEPS - 1)
     def _(t):
@@ -475,22 +473,19 @@
     one_step(STEPS - 1, True)
 
     def gather_quarter(q):
-        def one_tile(i, total):
+        @pl.loop(0, quarter)
+        def _(i):
             tile = q * quarter + i
-
-            @pl.loop(0, LANES // 32)
-            def _(g):
-                for v in range(4):
-                    taken = jnp.zeros((8, LANES), F32)
-                    for u in range(8):
-                        row = final_c[pl.ds(place[tile, g * 32 + v * 8 + u], 1), :]
-                        taken = jnp.where(sub == u, jnp.broadcast_to(row, (8, LANES)), taken)
-                    window = pl.ds(pl.multiple_of(g * 32 + v * 8, 8), 8)
-                    found[window, :] = taken * mask_v[tile, window, :]
-
-            return total + jnp.dot(parts_of(found[...]), pick_out[i], preferred_element_type=F32)
-
-        total = lax.fori_loop(0, quarter, one_tile, jnp.zeros((LANES, LANES), F32))
+            for g in range(LANES // 8):
+                taken = jnp.zeros((8, LANES), F32)
+                for u in range(8):
+                    row = final_c[pl.ds(place[tile, g * 8 + u], 1), :]
+                    taken = jnp.where(sub == u, jnp.broadcast_to(row, (8, LANES)), taken)
+                window = pl.ds(pl.multiple_of(i * LANES + g * 8, 8), 8)
+                found[window, :] = taken * mask_v[tile, pl.ds(g * 8, 8), :]
+
+        parts = [parts_of(found[pl.ds(i * LANES, LANES), :]) for i in range(quarter)]
+        total = jnp.dot(jnp.concatenate(parts, axis=1), pick_out[...], preferred_element_type=F32)
         turned = jnp.transpose(total)
         for i in range(quarter):
             picked[q, i] = turned[i * 8 : i * 8 + 8]
@@ -506,10 +501,11 @@
                         b * 8 : b * 8 + 8
                     ]
 
-    for p in range(1, 4):
+    @pl.loop(1, 5)
+    def _(p):
         gather_quarter(lax.rem(ens + p, 4))
-        picked_copy(p).start()
-    gather_quarter(ens)
+        pl.when(p < 4)(lambda: picked_copy(p).start())
+
     for i in range(quarter):
         all_picked[ens, i] = picked[ens, i]
     emit_rows(0, 6)
@@ -667,7 +663,7 @@
             jax.ShapeDtypeStruct((members * rows * tiles, LANES), F32),
             jax.ShapeDtypeStruct((members, columns), F32),
         ),
-        in_specs=[smem, anywhere, anywhere, anywhere, anywhere, anywhere, anywhere],
+        in_specs=[smem] + [pl.BlockSpec(memory_space=pltpu.HBM)] * 6,
         out_specs=(anywhere, vmem),
         scratch_shapes=[
             pltpu.VMEM((members * rows * tiles, LANES), F32),
@@ -678,7 +674,7 @@
             pltpu.VMEM((obs_tiles, LANES), jnp.int32),
             pltpu.SMEM((obs_tiles, LANES), jnp.int32),
             pltpu.VMEM((3 * LANES, 8 * LANES), jnp.bfloat16),
-            pltpu.VMEM((obs_tiles // 4, 3 * LANES, LANES), jnp.bfloat16),
+            pltpu.VMEM((obs_tiles // 4 * 3 * LANES, LANES), jnp.bfloat16),
             pltpu.VMEM((segment, LANES), F32),
             pltpu.VMEM((4,) + wide, F32),
             pltpu.VMEM((STEPS, rows, segment + 2 * EDGE, LANES), F32),
@@ -687,7 +683,7 @@
             pltpu.VMEM(wide, F32),
             pltpu.VMEM((rows * segment, LANES), F32),
             pltpu.VMEM((obs_tiles, LANES, LANES), F32),
-            pltpu.VMEM((LANES, LANES), F32),
+            pltpu.VMEM((obs_tiles // 4 * LANES, LANES), F32),
             pltpu.VMEM((members * rows * tiles, LANES), F32),
             pltpu.VMEM((4, members, columns), F32),
             pltpu.VMEM((4, members, obs_tiles // 4 * LANES), F32),

time: 72 us -> 63.8 us (0.89)
  Pallas kernels: 67.4 us -> 59.2 us
    pallas_call x1, Pallas kernels: 67.4 us -> 59.2 us  [local(): pl.pallas_call(functools.partial(kernel, slabs, tiles), out_shape=(jax.Sh...]
where the time goes in v3:
time: 63.8 us; the launch traced here: 63.6 us
  Pallas kernels  59.2 us (93%)
  local copies, waits for them, and re-layouts  3.81 us (6%)
  between operations  0.65 us (1%)
    pallas_call x1, Pallas kernels, local(): pl.pallas_call(functools.partial(kernel, slabs, tiles), out_shape=(jax.Sh...  59.2 us
    unnamed x4, local copies, waits for them, and re-layouts  3.81 us

profile of v3, /device:TPU:1, one launch (start us, length us, event | category | flops | bytes accessed | tf_op | source)
XLA Modules:
  0.0 63.6 jit_solution(10060566210879496296)
XLA Ops:
  0.6 59.2 %shard_map.86 = (f32[4096,128]{1,0:T(8,128)}, f32[8,4096]{1,0:T(8,128)}) custom-call(s32[32]{0:T(128)} %group_ref.1, s32[16,128]{1,0:T(8,128)} %bitcast.20, f32[4096,128]{1,0:T(8,128)} %bitcast.17, f32[256,8,128]{2,1,0:T(8,128)} %bitcast.19, f32[8,4096]{1,0:T(8,128)} %params_ref.1, f32[8,2048]{1,0:T(8,128)} %values_ref.1, f32[16,128]{1,0:T(8,128)} %bitcast.21), custom_call_target="tpu_custom_call" | custom-call | tf_op jit(solution)/shard_map/pallas_call | solution.py:660
  59.8 0.0 copy-start
  59.8 3.1 %copy.11 = f32[8,16,4096]{2,1,0:T(8,128)} copy(f32[8,16,4096]{2,1,0:T(8,128)} %bitcast.18) | data formatting | bytes 4194304
  63.0 0.0 copy-done
  63.0 0.7 %copy.12 = f32[8,4096]{1,0:T(8,128)} copy(f32[8,4096]{1,0:T(8,128)S(1)} %copy-done) | data formatting | bytes 262144
Async XLA Ops:
  59.8 3.2 %copy-start = (f32[8,4096]{1,0:T(8,128)S(1)}, f32[8,4096]{1,0:T(8,128)}, u32[]{:S(2)}) copy-start(f32[8,4096]{1,0:T(8,128)} %get-tuple-element.9) | copy-start | bytes 393220

commit v4 on v3

--- a/solution.py
+++ b/solution.py
@@ -550,17 +550,13 @@
                 device_id_type=MESH,
             )
 
-        @pl.loop(1, count)
-        def _(p):
-            copy(lax.rem(me + p, count), p).start()
-
+        copies = [copy(lax.rem(me + p, count), p) for p in range(1, count)]
+        for one in copies:
+            one.start()
         sums[me] = value
         meanwhile()
-
-        @pl.loop(1, count)
-        def _(p):
-            copy(lax.rem(me + p, count), p).wait()
-
+        for one in copies:
+            one.wait()
         total = sums[0]
         for i in range(1, count):
             total = total + sums[i]
@@ -571,6 +567,22 @@
     def rest_of_field():
         emit_rows(11, rows)
         field_store.start()
+        for p in range(1, 4):
+            params_copy(p).wait_send()
+            values_copy(p).wait_send()
+            picked_copy(p).wait_send()
+
+        @pl.loop(0, STEPS)
+        def _(t):
+            @pl.loop(0, CHUNKS)
+            def _(k):
+                @pl.when(has_right)
+                def _():
+                    halo_copy(t, 0, k).wait_send()
+
+                @pl.when(has_left)
+                def _():
+                    halo_copy(t, 1, k).wait_send()
 
     total = sum_over(
         packed,
@@ -624,23 +636,6 @@
         for s in range(4):
             value = value + solved[s] * moved[s, :, window]
         params_out[:, window] = value
-
-    for p in range(1, 4):
-        params_copy(p).wait_send()
-        values_copy(p).wait_send()
-        picked_copy(p).wait_send()
-
-    @pl.loop(0, STEPS)
-    def _(t):
-        @pl.loop(0, CHUNKS)
-        def _(k):
-            @pl.when(has_right)
-            def _():
-                halo_copy(t, 0, k).wait_send()
-
-            @pl.when(has_left)
-            def _():
-                halo_copy(t, 1, k).wait_send()
 
     field_store.wait()
 

time: 63.8 us -> 63.6 us (level)
  no operation moved by 1% of the time
where the time goes in v4:
time: 63.6 us; the launch traced here: 63.5 us
  Pallas kernels  59 us (93%)
  local copies, waits for them, and re-layouts  3.81 us (6%)
  between operations  0.65 us (1%)
    pallas_call x1, Pallas kernels, local(): pl.pallas_call(functools.partial(kernel, slabs, tiles), out_shape=(jax.Sh...  59 us
    unnamed x4, local copies, waits for them, and re-layouts  3.81 us

profile of v4, /device:TPU:1, one launch (start us, length us, event | category | flops | bytes accessed | tf_op | source)
XLA Modules:
  0.0 63.5 jit_solution(2222296270329985614)
XLA Ops:
  0.6 59.0 %shard_map.86 = (f32[4096,128]{1,0:T(8,128)}, f32[8,4096]{1,0:T(8,128)}) custom-call(s32[32]{0:T(128)} %group_ref.1, s32[16,128]{1,0:T(8,128)} %bitcast.20, f32[4096,128]{1,0:T(8,128)} %bitcast.17, f32[256,8,128]{2,1,0:T(8,128)} %bitcast.19, f32[8,4096]{1,0:T(8,128)} %params_ref.1, f32[8,2048]{1,0:T(8,128)} %values_ref.1, f32[16,128]{1,0:T(8,128)} %bitcast.21), custom_call_target="tpu_custom_call" | custom-call | tf_op jit(solution)/shard_map/pallas_call | solution.py:655
  59.7 0.0 copy-start
  59.7 3.1 %copy.11 = f32[8,16,4096]{2,1,0:T(8,128)} copy(f32[8,16,4096]{2,1,0:T(8,128)} %bitcast.18) | data formatting | bytes 4194304
  62.8 0.0 copy-done
  62.8 0.7 %copy.12 = f32[8,4096]{1,0:T(8,128)} copy(f32[8,4096]{1,0:T(8,128)S(1)} %copy-done) | data formatting | bytes 262144
Async XLA Ops:
  59.7 3.2 %copy-start = (f32[8,4096]{1,0:T(8,128)S(1)}, f32[8,4096]{1,0:T(8,128)}, u32[]{:S(2)}) copy-start(f32[8,4096]{1,0:T(8,128)} %get-tuple-element.9) | copy-start | bytes 393220
